TPU v7x, 1024 devices: a whole 8x8x8 slice. The times are simulated.
1024 devices in a mesh: fsdp: 128 (over x, y, z_lo), tp: 8 (over z_hi, core).
Axes of the slice: x: 8, y: 8, z: 8 (z_hi: 4, z_lo: 2; z = z_hi * 2 + z_lo), core: 2. Of those that a mesh axis runs over, the one named last changes fastest.
Arguments:
- acts: bfloat16 [32768, 128], P('fsdp'), may hold values from -24 to 24
- out_grad: bfloat16 [32768, 28672], P('fsdp', 'tp'), may hold values from -0.03125 to 0.03125
- moment: float32 [128, 28672], P('fsdp', 'tp'), may hold values from -4 to 4
- second: float32 [128, 28672], P('fsdp', 'tp'), may hold values from 0.01 to 1
- master: float32 [128, 28672], P('fsdp', 'tp'), may hold values from -0.5 to 0.5
- queries: bfloat16 [128, 64, 64, 128], P('fsdp', None, 'tp'), may hold values from -20 to 20
- cache_keys: bfloat16 [128, 1024, 8, 128], P('fsdp', None, 'tp'), may hold values from -6 to 6, as said below
- cache_values: bfloat16 [128, 1024, 8, 128], P('fsdp', None, 'tp'), may hold values from -6 to 6
- tree_keys: bfloat16 [128, 64, 8, 128], P('fsdp', None, 'tp'), may hold values from -6 to 6
- tree_values: bfloat16 [128, 64, 8, 128], P('fsdp', None, 'tp'), may hold values from -6 to 6
- parents: int32 [128, 64], P('fsdp'), may hold values from 0 to 62, as said below
- lengths: int32 [128], P('fsdp'), may hold values from 256 to 1024, as said below
- residual: bfloat16 [128, 64, 128], P('fsdp'), may hold values from -6 to 6
- out_proj: bfloat16 [8192, 128], P('tp'), may hold values from -0.75 to 0.75
Outputs:
- moment_new: float32 [128, 28672], P('fsdp', 'tp')
- second_new: float32 [128, 28672], P('fsdp', 'tp')
- master_new: float32 [128, 28672], P('fsdp', 'tp')
- proposal: bfloat16 [128, 64, 28672], P('fsdp', None, 'tp')
Inputs may be any that keep to these rules, and one draw needn't show every extreme that they name: `cache_keys`: custom bfloat16 keys. parents[r, 0] = 0 (the root); for i >= 1, parents[r, i] < i. `lengths`: request 0 holds exactly 1024 cached tokens.
All inputs are finite; a program needn't handle non-finite values.
Results may differ from a plain program's by a relative error of at most 0.008.
Values may be sent and summed in bfloat16 or wider, within the bound.
A program may use at most 32 MiB of HBM per device.

v0:
```python
import jax
import jax.numpy as jnp
from jax import lax
from jax.sharding import PartitionSpec as P

beta_one = 0.9
beta_two = 0.95
adam_eps = 1e-08
learn_rate = 0.001
weight_decay = 0.1
adam_count = 10
masked_score = -1e30


def ancestry(parent_row):
    nodes = parent_row.shape[0]
    positions = jnp.arange(nodes, dtype=jnp.int32)
    links = ((positions[None, :] == parent_row[:, None]) & (positions[:, None] > 0)).astype(
        jnp.float32
    )
    identity_matrix = jnp.eye(nodes, dtype=jnp.float32)
    reach = identity_matrix + links
    for sweep in range(max(1, (nodes - 1).bit_length())):
        reach = jnp.minimum(jnp.dot(reach, reach, preferred_element_type=jnp.float32), 1.0)
    return reach


def tree_attend(query, cache_k, cache_v, tree_k, tree_v, length, parent_row):
    nodes, heads, depth = query.shape
    kv_heads = cache_k.shape[1]
    group = heads // kv_heads
    score_scale = depth ** (-0.5)
    grouped = query.reshape(nodes, kv_heads, group, depth)
    cache_scores = (
        jnp.einsum("nkgd,ckd->kgnc", grouped, cache_k, preferred_element_type=jnp.float32)
        * score_scale
    )
    tree_scores = (
        jnp.einsum("nkgd,mkd->kgnm", grouped, tree_k, preferred_element_type=jnp.float32)
        * score_scale
    )
    live = jnp.arange(cache_k.shape[0], dtype=jnp.int32) < length
    cache_scores = jnp.where(live, cache_scores, masked_score)
    tree_scores = jnp.where(ancestry(parent_row) > 0.5, tree_scores, masked_score)
    row_top = jnp.maximum(
        jnp.max(cache_scores, -1, keepdims=True), jnp.max(tree_scores, -1, keepdims=True)
    )
    cache_exp = jnp.exp(cache_scores - row_top)
    tree_exp = jnp.exp(tree_scores - row_top)
    total = jnp.sum(cache_exp, -1, keepdims=True) + jnp.sum(tree_exp, -1, keepdims=True)
    cache_weights = (cache_exp / total).astype(jnp.bfloat16)
    tree_weights = (tree_exp / total).astype(jnp.bfloat16)
    mixed = jnp.einsum("kgnc,ckd->nkgd", cache_weights, cache_v, preferred_element_type=jnp.float32)
    mixed = mixed + jnp.einsum(
        "kgnm,mkd->nkgd", tree_weights, tree_v, preferred_element_type=jnp.float32
    )
    return mixed.reshape(nodes, heads * depth).astype(jnp.bfloat16)


def local(
    acts,
    out_grad,
    moment,
    second,
    master,
    queries,
    cache_keys,
    cache_values,
    tree_keys,
    tree_values,
    parents,
    lengths,
    residual,
    out_proj,
):
    requests, nodes = (queries.shape[0], queries.shape[1])

    def attend_one(items):
        return tree_attend(*items)

    columns = acts
    gradient = lax.psum_scatter(
        lax.dot_general(
            columns, out_grad, (((0,), (0,)), ((), ())), preferred_element_type=jnp.float32
        ),
        "fsdp",
        scatter_dimension=0,
        tiled=True,
    )
    attended = lax.map(
        attend_one, (queries, cache_keys, cache_values, tree_keys, tree_values, lengths, parents)
    )
    head_term = jnp.dot(
        attended.reshape(requests * nodes, -1), out_proj, preferred_element_type=jnp.float32
    )
    head_out = lax.psum(head_term, "tp")
    hidden = (residual.reshape(requests * nodes, -1).astype(jnp.float32) + head_out).astype(
        jnp.bfloat16
    )
    moment_new = beta_one * moment + (1.0 - beta_one) * gradient
    second_new = beta_two * second + (1.0 - beta_two) * gradient * gradient
    corr_one = 1.0 - beta_one**adam_count
    corr_two = 1.0 - beta_two**adam_count
    direction = moment_new / corr_one / (jnp.sqrt(second_new / corr_two) + adam_eps)
    master_new = master - learn_rate * (direction + weight_decay * master)
    rollout = master_new.astype(jnp.bfloat16)
    columns = hidden
    summed = jnp.dot(
        columns,
        lax.all_gather(rollout, "fsdp", axis=0, tiled=True),
        preferred_element_type=jnp.float32,
    )
    proposal = summed.astype(jnp.bfloat16).reshape(requests, nodes, -1)
    return (moment_new, second_new, master_new, proposal)


def solution(mesh):
    in_specs = (
        P("fsdp", None),
        P("fsdp", "tp"),
        P("fsdp", "tp"),
        P("fsdp", "tp"),
        P("fsdp", "tp"),
        P("fsdp", None, "tp", None),
        P("fsdp", None, "tp", None),
        P("fsdp", None, "tp", None),
        P("fsdp", None, "tp", None),
        P("fsdp", None, "tp", None),
        P("fsdp", None),
        P("fsdp"),
        P("fsdp", None, None),
        P("tp", None),
    )
    out_specs = (P("fsdp", "tp"), P("fsdp", "tp"), P("fsdp", "tp"), P("fsdp", None, "tp"))
    return jax.shard_map(local, mesh=mesh, in_specs=in_specs, out_specs=out_specs, check_vma=False)
```

profile of v0, /device:TPU:8, one launch (start us, length us, event | category | flops | bytes accessed | tf_op | source)
XLA Modules:
  0.0 1525.5 jit_solution(4502513307225057109)
XLA Ops:
  7.2 0.0 copy-start
  7.2 0.0 copy-start.11
  7.2 0.0 copy-start.1
  7.2 0.0 copy-start.5
  7.2 0.0 all-reduce.3.cloned.1.call-start
  7.3 1.4 copy-done
  8.7 2.5 fusion.52
  11.2 0.0 copy-start.2
  11.2 0.0 all-reduce.3.cloned.1.call-update
  11.9 0.0 copy-done.11
  11.9 0.4 convolution_minimum_fusion.4
  12.3 0.3 convolution_minimum_fusion.2
  12.5 0.3 fusion.7
  12.8 0.1 copy.28
  12.9 0.0 copy-done.1
  12.9 0.0 copy-done.5
  12.9 0.3 fusion.51
  13.2 0.0 copy-done.2
  13.2 0.0 copy-start.9
  13.2 0.5 bitcast_reduce_fusion
  13.8 0.1 fusion.15
  13.8 0.5 fusion.2
  14.4 0.0 copy-done.9
  14.4 0.0 copy-start.10
  14.4 0.0 copy-start.3
  14.4 0.0 copy-start.6
  14.4 0.0 copy-start.7
  14.4 0.0 copy-start.8
  14.5 0.6 fusion.8
  15.1 0.0 copy-done.10
  15.1 0.0 copy-start.4
  15.1 0.2 fusion.6
  15.4 0.1 copy.31
  15.5 1.3 dynamic-slice
  16.8 0.0 copy-done.3
  16.8 0.2 fusion.16
  16.9 41.0 %psum.7 = f32[64,128]{1,0:T(8,128)S(1)} all-reduce(f32[64,128]{1,0:T(8,128)S(1)} %fusion.16), channel_id=1, replica_groups=mesh['fsdp'=128,'tp'=8] {'tp'}, use_global_device_ids=true, to_apply=%region_5.6 | all-reduce | flops 8192 | bytes 65536 | tf_op jit(solution)/shard_map/psum | solution.py:96
  57.9 1144.0 %all-reduce.3.cloned.1.call-done = f32[128,3584]{1,0:T(8,128)} async-done(((f32[128,3584]{1,0:T(8,128)}), f32[128,3584]{1,0:T(8,128)}) %all-reduce.3.cloned.1.call-update) | async-done | bytes 1835024
  1201.9 0.0 copy-done.6
  1201.9 0.0 copy-done.7
  1202.0 0.0 copy-done.8
  1202.0 2.3 convert_bitcast_fusion
  1204.2 313.3 %all-gather = bf16[128,1,3584]{2,1,0:T(2,128)(2,1)S(1)} all-gather(bf16[1,1,3584]{2,1,0:T(2,128)(2,1)S(1)} %get-tuple-element.22), channel_id=1, replica_groups=mesh['fsdp'=128,'tp'=8] {'fsdp'}, dimensions={0}, use_global_device_ids=true | all-gather | bytes 924672 | tf_op jit(solution)/shard_map/all_gather | solution.py:110
  1517.6 0.0 copy-done.4
  1517.6 1.0 fusion
  (4 shorter events, 0.0 us)
Async XLA Ops:
  7.2 1.5 copy-start
  7.2 4.7 copy-start.11
  7.2 5.7 copy-start.1
  7.2 5.7 copy-start.5
  7.2 1194.7 %all-reduce.3.cloned.1.call-start = ((), (), s32[]{:S(2)}) async-start(), calls=%async_computation | async-start | bytes 3670016
  11.2 2.0 copy-start.2
  13.2 1.2 copy-start.9
  14.4 0.7 copy-start.10
  14.4 2.3 copy-start.3
  14.4 1187.5 %copy-start.6 = (f32[1,3584]{1,0:T(1,128)S(1)}, f32[1,3584]{1,0:T(1,128)}, u32[]{:S(2)}) copy-start(f32[1,3584]{1,0:T(1,128)} %param.18) | copy-start | bytes 43012
  14.4 1187.5 %copy-start.7 = (f32[1,3584]{1,0:T(1,128)S(1)}, f32[1,3584]{1,0:T(1,128)}, u32[]{:S(2)}) copy-start(f32[1,3584]{1,0:T(1,128)} %param.17) | copy-start | bytes 43012
  14.4 1187.5 %copy-start.8 = (f32[1,3584]{1,0:T(1,128)S(1)}, f32[1,3584]{1,0:T(1,128)}, u32[]{:S(2)}) copy-start(f32[1,3584]{1,0:T(1,128)} %param.16) | copy-start | bytes 43012
  15.1 1502.4 %copy-start.4 = (bf16[1,64,128]{2,1,0:T(8,128)(2,1)S(1)}, bf16[1,64,128]{2,1,0:T(8,128)(2,1)}, u32[]{:S(2)}) copy-start(bf16[1,64,128]{2,1,0:T(8,128)(2,1)} %param.26) | copy-start | bytes 49156
Sparse Core Ops, SparseCore 0:
  11.5 1190.3 all-reduce.2
where the time goes:
time: 1530 us
  waiting for transfers between devices  1140 us (75%)
  blocking collectives  354 us (23%)
    unnamed x2, waiting for transfers between devices  1140 us
    all_gather x1, blocking collectives, local(): lax.all_gather(rollout, 'fsdp', axis=0, tiled=True)  313 us
    psum x1, blocking collectives, local(): head_out = lax.psum(head_term, 'tp')  41 us
  transfers between devices with their start and end apart: 1, of which 1 were waited for; matrix products, arithmetic and copies ran while one was open for 0% of the time, Pallas kernels for 0%

commit v1 on v0

v1 whole, which is shorter than its diff:
```python
import functools

import jax
import jax.numpy as jnp
from jax import lax
from jax.experimental import pallas as pl
from jax.experimental.pallas import tpu as pltpu
from jax.sharding import PartitionSpec as P

beta_one = 0.9
beta_two = 0.95
adam_eps = 1e-08
learn_rate = 0.001
weight_decay = 0.1
adam_count = 10
masked_score = -1e30

MESH = pl.DeviceIdType.MESH
LANES = 128
GRIDS = {128: (8, 8, 2), 32: (4, 4, 2), 16: (4, 4, 1), 8: (2, 2, 2)}


def nt_dot(a, b):
    return lax.dot_general(a, b, (((1,), (1,)), ((), ())), preferred_element_type=jnp.float32)


def dot(a, b):
    return jnp.dot(a, b, preferred_element_type=jnp.float32)


def kernel(
    cfg,
    acts_h,
    og_h,
    mom_h,
    sec_h,
    mas_h,
    q_h,
    k_h,
    v_h,
    tk_h,
    tv_h,
    par_h,
    len_s,
    res_h,
    op_h,
    mom_o,
    sec_o,
    mas_o,
    prop_o,
    acts,
    og,
    opt,
    q,
    k,
    v,
    tk,
    tv,
    par,
    res,
    op,
    grad,
    rs_out,
    rs_in,
    tile_f,
    tile_out,
    tile_in,
    row_all,
    roll,
    qf,
    ht,
    pair_in,
    quad,
    hid,
    opt_new,
    own,
    stage,
    load_sem,
    store_sem,
    rs_send,
    rs_recv,
    ex_send,
    ex_recv,
    row_send,
    row_recv,
    ag_send,
    ag_recv,
    tp_send,
    tp_recv,
):
    nx, ny, nz, nq, chunks = cfg
    rows = acts.shape[1]
    width = grad.shape[-1]
    tiles = width // LANES * chunks
    pad = tile_f.shape[0] // (rows // nx)
    nodes = res.shape[0]
    heads = q.shape[0] // nodes
    half_nodes = nodes // 2

    f = lax.axis_index("fsdp")
    t = lax.axis_index("tp")
    x, y, z = f // (ny * nz), lax.rem(f // nz, ny), lax.rem(f, nz)
    core, zh = lax.rem(t, 2), t // 2
    sides = (nx, ny)
    pos = (x, y)
    group = (ny * nz, nx * nz)
    mine = (y * nz + z, x * nz + z)

    def ring_peer(a, step):
        if a == 0:
            return (lax.rem(x + step + nx, nx) * ny + y) * nz + z
        return (x * ny + lax.rem(y + step + ny, ny)) * nz + z

    def group_peer(a, j):
        if a == 0:
            return x * (ny * nz) + j
        return ((j // nz) * ny + y) * nz + lax.rem(j, nz)

    loads = {}

    def load(name, src, dst):
        copy = pltpu.make_async_copy(src, dst, load_sem.at[len(loads)])
        copy.start()
        loads[name] = copy

    load("acts", acts_h, acts)
    for c in range(chunks):
        for a in range(2):
            base = (a * chunks + c) * width
            load(("og", a, c), og_h.at[:, pl.ds(base, width)], og.at[a, c])
    load("par", par_h, par)
    load("q", q_h, q)
    load("tk", tk_h, tk)
    load("k", k_h, k)
    load("v", v_h, v)
    load("tv", tv_h, tv)
    load("op", op_h, op)
    load("res", res_h, res)
    load("mom", mom_h, opt.at[0])
    load("sec", sec_h, opt.at[1])
    load("mas", mas_h, opt.at[2])

    barrier = pltpu.get_barrier_semaphore()
    count = 0
    for kk in range(1, group[0]):
        j = lax.rem(mine[0] + kk, group[0])
        pl.semaphore_signal(barrier, inc=1, device_id=(group_peer(0, j), t), device_id_type=MESH)
        count += 1
    for xx in range(1, nx):
        for zz in range(nz):
            j = lax.rem(x + xx, nx) * nz + zz
            pl.semaphore_signal(barrier, inc=1, device_id=(group_peer(1, j), t), device_id_type=MESH)
            count += 1
    sibling = zh * 2 + 1 - core
    pl.semaphore_signal(barrier, inc=1, device_id=(f, sibling), device_id_type=MESH)
    count += 1
    for kk in range(1, nq):
        peer = lax.rem(zh + kk, nq) * 2 + core
        pl.semaphore_signal(barrier, inc=1, device_id=(f, peer), device_id_type=MESH)
        count += 1

    tile_f[...] = jnp.zeros_like(tile_f)

    row_at = lax.broadcasted_iota(jnp.int32, (rows, rows), 0)
    col_at = lax.broadcasted_iota(jnp.int32, (rows, rows), 1)
    py, px, pz = row_at // (nx * nz), lax.rem(row_at // nz, nx), lax.rem(row_at, nz)
    swap = (col_at == (px * ny + py) * nz + pz).astype(jnp.bfloat16)
    same = (col_at == row_at).astype(jnp.bfloat16)
    loads["acts"].wait()
    acts_t = [nt_dot(same, acts[...]).astype(jnp.bfloat16), nt_dot(swap, acts[...]).astype(jnp.bfloat16)]

    started = []

    def block(a, target):
        return pl.ds(pl.multiple_of(target * (rows // sides[a]), rows // sides[a]), rows // sides[a])

    def rs_copy(a, d, s, c):
        sign = 1 - 2 * d
        return pltpu.make_async_remote_copy(
            src_ref=rs_out.at[a, d, s, c],
            dst_ref=rs_in.at[a, d, s, c],
            send_sem=rs_send.at[a, d, s, c],
            recv_sem=rs_recv.at[a, d, s, c],
            device_id=(ring_peer(a, sign), t),
            device_id_type=MESH,
        )

    def rs_step(a, d, s, c):
        n = sides[a]
        sign = 1 - 2 * d
        target = lax.rem(pos[a] + sign * (n // 2 - s) + n, n)
        value = grad[a, c, block(a, target), :]
        if s > 1 or (s == 1 and c % 2 == d):
            rs_copy(a, d, s - 1, c).wait_recv()
            value = value + rs_in[a, d, s - 1, c].astype(jnp.float32)
        rs_out[a, d, s, c] = value.astype(jnp.bfloat16)
        copy = rs_copy(a, d, s, c)
        copy.start()
        started.append(copy)

    first = True
    for c in range(chunks):
        for a in range(2):
            loads[("og", a, c)].wait()
            grad[a, c] = dot(acts_t[a], og[a, c])
            if first:
                pl.semaphore_wait(barrier, count)
                first = False
            rs_step(a, c % 2, 0, c)

    loads["par"].wait()
    j_at = lax.broadcasted_iota(jnp.int32, (nodes, nodes), 0)
    i_at = lax.broadcasted_iota(jnp.int32, (nodes, nodes), 1)
    links = ((par[...] == j_at) & (i_at > 0)) | (i_at == j_at)
    reach = links.astype(jnp.bfloat16)
    for _ in range(max(1, (nodes - 1).bit_length())):
        reach = jnp.minimum(dot(reach, reach), 1.0).astype(jnp.bfloat16)
    pick_row = lax.broadcasted_iota(jnp.int32, (2 * nodes, nodes), 0)
    pick_col = lax.broadcasted_iota(jnp.int32, (2 * nodes, nodes), 1)
    pick = (lax.rem(pick_row, nodes) == pick_col).astype(jnp.bfloat16)
    admitted = nt_dot(pick, reach) > 0.5
    loads["q"].wait()
    qf[...] = q[...].astype(jnp.float32)

    depth = q.shape[1]
    scale = depth ** (-0.5)

    def attend(u):
        if u == 0:
            loads["tk"].wait()
            loads["k"].wait()
        pair = jnp.concatenate(
            [qf[pl.ds(2 * u + e, nodes, stride=heads), :] for e in range(2)], axis=0
        ).astype(jnp.bfloat16)
        s_cache = nt_dot(pair, k[...])
        s_tree = nt_dot(pair, tk[...])
        live = lax.broadcasted_iota(jnp.int32, s_cache.shape, 1) < len_s[0]
        s_cache = jnp.where(live, s_cache, masked_score)
        s_tree = jnp.where(admitted, s_tree, masked_score)
        top = jnp.maximum(
            jnp.max(s_cache, axis=1, keepdims=True), jnp.max(s_tree, axis=1, keepdims=True)
        )
        e_cache = jnp.exp((s_cache - top) * scale)
        e_tree = jnp.exp((s_tree - top) * scale)
        total = jnp.sum(e_cache, axis=1, keepdims=True) + jnp.sum(e_tree, axis=1, keepdims=True)
        if u == 0:
            loads["v"].wait()
            loads["tv"].wait()
            loads["op"].wait()
        mixed = dot(e_cache.astype(jnp.bfloat16), v[...]) + dot(e_tree.astype(jnp.bfloat16), tv[...])
        mixed = (mixed / total).astype(jnp.bfloat16)
        add = dot(mixed[:nodes], op[pl.ds(2 * u * depth, depth), :]) + dot(
            mixed[nodes:], op[pl.ds((2 * u + 1) * depth, depth), :]
        )
        if u == 0:
            ht[...] = add
        else:
            ht[...] += add

    unit = 0
    units = heads // 2
    steps = max(nx, ny) // 2
    for s in range(1, steps):
        for c in range(chunks):
            for a in range(2):
                for d in range(2):
                    if s < sides[a] // 2:
                        rs_step(a, d, s, c)
        if unit < units:
            attend(unit)
            unit += 1
    while unit < units:
        attend(unit)
        unit += 1

    own_nodes = pl.ds(pl.multiple_of(core * half_nodes, half_nodes), half_nodes)
    other_nodes = pl.ds(pl.multiple_of((1 - core) * half_nodes, half_nodes), half_nodes)
    pair_copy = pltpu.make_async_remote_copy(
        src_ref=ht.at[other_nodes],
        dst_ref=pair_in,
        send_sem=tp_send.at[0],
        recv_sem=tp_recv.at[0],
        device_id=(f, sibling),
        device_id_type=MESH,
    )
    pair_copy.start()

    ex_copies = []
    for a in range(2):
        n = sides[a]
        last = n // 2 - 1
        for c in range(chunks):
            value = grad[a, c, block(a, pos[a]), :]
            for d in range(2):
                if last > 0 or c % 2 == d:
                    rs_copy(a, d, last, c).wait_recv()
                    value = value + rs_in[a, d, last, c].astype(jnp.float32)
            for e in range(width // LANES):
                at = c * (width // LANES) + e
                tile_f[pl.ds(at, group[a], stride=pad), :] = value[:, e * LANES : (e + 1) * LANES]
        tile_out[a] = tile_f[...].astype(jnp.bfloat16).reshape(group[a], pad, LANES)
        own[a] = tile_f[pl.ds(pl.multiple_of(mine[a] * pad, pad), pad), :]
        for kk in range(1, group[a]):
            j = lax.rem(mine[a] + kk, group[a])
            copy = pltpu.make_async_remote_copy(
                src_ref=tile_out.at[a, j],
                dst_ref=tile_in.at[a, kk - 1],
                send_sem=ex_send.at[a],
                recv_sem=ex_recv.at[a],
                device_id=(group_peer(a, j), t),
                device_id_type=MESH,
            )
            copy.start()
            ex_copies.append(copy)

    pair_copy.wait_recv()
    quad[zh] = ht[own_nodes, :] + pair_in[...]
    quad_copies = []
    for kk in range(1, nq):
        copy = pltpu.make_async_remote_copy(
            src_ref=quad.at[zh],
            dst_ref=quad.at[zh],
            send_sem=tp_send.at[kk],
            recv_sem=tp_recv.at[kk],
            device_id=(f, lax.rem(zh + kk, nq) * 2 + core),
            device_id_type=MESH,
        )
        copy.start()
        quad_copies.append(copy)

    for name in ("mom", "sec", "mas"):
        loads[name].wait()
    corr_one = 1.0 - beta_one**adam_count
    corr_two = 1.0 - beta_two**adam_count
    for a in range(2):
        pltpu.make_async_copy(
            tile_in.at[a, pl.ds(0, group[a] - 1)], tile_in.at[a, pl.ds(0, group[a] - 1)], ex_recv.at[a]
        ).wait()
        g = own[a]
        for kk in range(group[a] - 1):
            g = g + tile_in[a, kk].astype(jnp.float32)
        g = g[:tiles]
        part = pl.ds(a * tiles, tiles)
        moment_new = beta_one * opt[0, part, :] + (1.0 - beta_one) * g
        second_new = beta_two * opt[1, part, :] + (1.0 - beta_two) * g * g
        direction = moment_new / corr_one / (jnp.sqrt(second_new / corr_two) + adam_eps)
        master = opt[2, part, :]
        master_new = master - learn_rate * (direction + weight_decay * master)
        fill = jnp.zeros((pad - tiles, LANES), jnp.float32)
        row_all[a, mine[a]] = jnp.concatenate([master_new, fill], axis=0).astype(jnp.bfloat16)
        for kk in range(1, group[a]):
            j = lax.rem(mine[a] + kk, group[a])
            copy = pltpu.make_async_remote_copy(
                src_ref=row_all.at[a, mine[a]],
                dst_ref=row_all.at[a, mine[a]],
                send_sem=row_send.at[a],
                recv_sem=row_recv.at[a],
                device_id=(group_peer(a, j), t),
                device_id_type=MESH,
            )
            copy.start()
        opt_new[0, part, :] = moment_new
        opt_new[1, part, :] = second_new
        opt_new[2, part, :] = master_new

    stores = []

    def store(src, dst):
        copy = pltpu.make_async_copy(src, dst, store_sem.at[len(stores)])
        copy.start()
        stores.append(copy)

    store(opt_new.at[0], mom_o)
    store(opt_new.at[1], sec_o)
    store(opt_new.at[2], mas_o)

    loads["res"].wait()
    for copy in quad_copies:
        copy.wait_recv()
    head_out = quad[0]
    for kk in range(1, nq):
        head_out = head_out + quad[kk]
    hid[own_nodes, :] = (res[own_nodes, :].astype(jnp.float32) + head_out).astype(jnp.bfloat16)
    hid_copy = pltpu.make_async_remote_copy(
        src_ref=hid.at[own_nodes],
        dst_ref=hid.at[own_nodes],
        send_sem=tp_send.at[nq],
        recv_sem=tp_recv.at[nq],
        device_id=(f, sibling),
        device_id_type=MESH,
    )
    hid_copy.start()

    def ag_copy(a, d, s, c):
        n = sides[a]
        sign = 1 - 2 * d
        owner = lax.rem(pos[a] - sign * s + n, n)
        ref = roll.at[a, c, block(a, owner)]
        return pltpu.make_async_remote_copy(
            src_ref=ref,
            dst_ref=ref,
            send_sem=ag_send.at[a, d, s, c],
            recv_sem=ag_recv.at[a, d, s, c],
            device_id=(ring_peer(a, sign), t),
            device_id_type=MESH,
        )

    def ag_used(a, d, s, c):
        return s < sides[a] // 2 - 1 or (s == sides[a] // 2 - 1 and c % 2 == d)

    def ag_wait(a, d, s, c):
        n = sides[a]
        sign = 1 - 2 * d
        owner = lax.rem(pos[a] - sign * (s + 1) + n, n)
        ref = roll.at[a, c, block(a, owner)]
        pltpu.make_async_remote_copy(
            src_ref=ref,
            dst_ref=ref,
            send_sem=ag_send.at[a, d, s, c],
            recv_sem=ag_recv.at[a, d, s, c],
            device_id=(ring_peer(a, sign), t),
            device_id_type=MESH,
        ).wait_recv()

    def ag_start(a, d, s, c):
        copy = ag_copy(a, d, s, c)
        copy.start()
        started.append(copy)

    for a in range(2):
        pltpu.make_async_copy(
            row_all.at[a, pl.ds(0, group[a] - 1)], row_all.at[a, pl.ds(0, group[a] - 1)], row_recv.at[a]
        ).wait()
        tile_f[...] = row_all[a].astype(jnp.float32).reshape(group[a] * pad, LANES)
        for c in range(chunks):
            for e in range(width // LANES):
                at = c * (width // LANES) + e
                roll[a, c, block(a, pos[a]), pl.ds(e * LANES, LANES)] = tile_f[
                    pl.ds(at, group[a], stride=pad), :
                ].astype(jnp.bfloat16)
            for d in range(2):
                if ag_used(a, d, 0, c):
                    ag_start(a, d, 0, c)
    for s in range(1, steps):
        for c in range(chunks):
            for a in range(2):
                for d in range(2):
                    if ag_used(a, d, s - 1, c):
                        ag_wait(a, d, s - 1, c)
                        if ag_used(a, d, s, c):
                            ag_start(a, d, s, c)

    hid_copy.wait_recv()
    hidden = hid[...]
    hiddens = (hidden, nt_dot(hidden, swap).astype(jnp.bfloat16))

    for c in range(chunks):
        for a in range(2):
            for d in range(2):
                last = sides[a] // 2 - 1
                if ag_used(a, d, last, c):
                    ag_wait(a, d, last, c)
            stage[a, c] = dot(hiddens[a], roll[a, c]).astype(jnp.bfloat16)
            store(stage.at[a, c], prop_o.at[:, pl.ds((a * chunks + c) * width, width)])

    for copy in started:
        copy.wait_send()
    for a in range(2):
        pltpu.make_async_copy(
            tile_out.at[a, pl.ds(0, group[a] - 1)], tile_out.at[a, pl.ds(0, group[a] - 1)], ex_send.at[a]
        ).wait()
        pltpu.make_async_copy(
            row_all.at[a, pl.ds(0, group[a] - 1)], row_all.at[a, pl.ds(0, group[a] - 1)], row_send.at[a]
        ).wait()
    pair_copy.wait_send()
    for copy in quad_copies:
        copy.wait_send()
    hid_copy.wait_send()
    for copy in stores:
        copy.wait()


def local(
    acts,
    out_grad,
    moment,
    second,
    master,
    queries,
    cache_keys,
    cache_values,
    tree_keys,
    tree_values,
    parents,
    lengths,
    residual,
    out_proj,
    *,
    grid,
    nq,
):
    nx, ny, nz = grid
    chunks = 2
    rows = acts.shape[1]
    columns = out_grad.shape[1]
    width = columns // (2 * chunks)
    tiles = width // LANES * chunks
    pad = -(-tiles // 16) * 16
    nodes, heads, depth = queries.shape[1:]
    cache = cache_keys.shape[1]
    side = ny * nz
    steps = nx // 2
    bf16, f32 = jnp.bfloat16, jnp.float32
    any_spec = pl.BlockSpec(memory_space=pl.ANY)
    dma = pltpu.SemaphoreType.DMA
    moment_new, second_new, master_new, proposal = pl.pallas_call(
        functools.partial(kernel, (nx, ny, nz, nq, chunks)),
        out_shape=[jax.ShapeDtypeStruct((2 * tiles, LANES), f32)] * 3
        + [jax.ShapeDtypeStruct((nodes, columns), bf16)],
        in_specs=[any_spec] * 11 + [pl.BlockSpec(memory_space=pltpu.SMEM)] + [any_spec] * 2,
        out_specs=[any_spec] * 4,
        scratch_shapes=[
            pltpu.VMEM(acts.shape, bf16),
            pltpu.VMEM((2, chunks, acts.shape[0], width), bf16),
            pltpu.VMEM((3, 2 * tiles, LANES), f32),
            pltpu.VMEM((nodes * heads, depth), bf16),
            pltpu.VMEM((cache, depth), bf16),
            pltpu.VMEM((cache, depth), bf16),
            pltpu.VMEM((nodes, depth), bf16),
            pltpu.VMEM((nodes, depth), bf16),
            pltpu.VMEM((1, nodes), jnp.int32),
            pltpu.VMEM((nodes, rows), bf16),
            pltpu.VMEM(out_proj.shape, bf16),
            pltpu.VMEM((2, chunks, rows, width), f32),
            pltpu.VMEM((2, 2, steps, chunks, side, width), bf16),
            pltpu.VMEM((2, 2, steps, chunks, side, width), bf16),
            pltpu.VMEM((side * pad, LANES), f32),
            pltpu.VMEM((2, side, pad, LANES), bf16),
            pltpu.VMEM((2, side - 1, pad, LANES), bf16),
            pltpu.VMEM((2, side, pad, LANES), bf16),
            pltpu.VMEM((2, chunks, rows, width), bf16),
            pltpu.VMEM((nodes * heads, depth), f32),
            pltpu.VMEM((nodes, rows), f32),
            pltpu.VMEM((nodes // 2, rows), f32),
            pltpu.VMEM((nq, nodes // 2, rows), f32),
            pltpu.VMEM((nodes, rows), bf16),
            pltpu.VMEM((3, 2 * tiles, LANES), f32),
            pltpu.VMEM((2, pad, LANES), f32),
            pltpu.VMEM((2, chunks, nodes, width), bf16),
            dma((12 + 2 * chunks,)),
            dma((3 + 2 * chunks,)),
            dma((2, 2, steps, chunks)),
            dma((2, 2, steps, chunks)),
            dma((2,)),
            dma((2,)),
            dma((2,)),
            dma((2,)),
            dma((2, 2, steps, chunks)),
            dma((2, 2, steps, chunks)),
            dma((nq + 1,)),
            dma((nq + 1,)),
        ],
        compiler_params=pltpu.CompilerParams(
            collective_id=0, has_side_effects=True, vmem_limit_bytes=44 * 1024 * 1024
        ),
    )(
        acts,
        out_grad,
        moment.reshape(2 * tiles, LANES),
        second.reshape(2 * tiles, LANES),
        master.reshape(2 * tiles, LANES),
        queries.reshape(nodes * heads, depth),
        cache_keys.reshape(cache, depth),
        cache_values.reshape(cache, depth),
        tree_keys.reshape(nodes, depth),
        tree_values.reshape(nodes, depth),
        parents,
        lengths,
        residual.reshape(nodes, rows),
        out_proj,
    )
    return (
        moment_new.reshape(moment.shape),
        second_new.reshape(second.shape),
        master_new.reshape(master.shape),
        proposal.reshape(1, nodes, columns),
    )


def solution(mesh):
    in_specs = (
        P("fsdp", None),
        P("fsdp", "tp"),
        P("fsdp", "tp"),
        P("fsdp", "tp"),
        P("fsdp", "tp"),
        P("fsdp", None, "tp", None),
        P("fsdp", None, "tp", None),
        P("fsdp", None, "tp", None),
        P("fsdp", None, "tp", None),
        P("fsdp", None, "tp", None),
        P("fsdp", None),
        P("fsdp"),
        P("fsdp", None, None),
        P("tp", None),
    )
    out_specs = (P("fsdp", "tp"), P("fsdp", "tp"), P("fsdp", "tp"), P("fsdp", None, "tp"))
    body = functools.partial(local, grid=GRIDS[mesh.shape["fsdp"]], nq=mesh.shape["tp"] // 2)
    return jax.shard_map(body, mesh=mesh, in_specs=in_specs, out_specs=out_specs, check_vma=False)
```

time: 1530 us -> 77.5 us (0.05)
  the two profiles are of different devices: /device:TPU:8 before, /device:TPU:6 now
where the time goes in v1:
time: 77.5 us; the launch traced here: 76.9 us
  Pallas kernels  62.4 us (81%)
  local copies, waits for them, and re-layouts  10.9 us (14%)
  other arithmetic  2.26 us (3%)
  between operations  1.31 us (2%)
    pallas_call x1, Pallas kernels, local(): pl.pallas_call(functools.partial(kernel, (nx, ny, nz, nq, chunks)), out_s...  62.4 us
    unnamed x22, local copies, waits for them, and re-layouts  10.3 us
    unnamed x3, other arithmetic  2.26 us

profile of v1, /device:TPU:6, one launch (start us, length us, event | category | flops | bytes accessed | tf_op | source)
XLA Modules:
  0.0 76.9 jit_solution(5687546281587948097)
XLA Ops:
  1.3 0.8 reduce
  2.0 0.8 reduce.1
  2.8 0.8 reduce.2
  3.5 0.0 copy-start
  3.6 1.5 %copy-done = bf16[256,3584]{1,0:T(8,128)(2,1)S(1)} copy-done((bf16[256,3584]{1,0:T(8,128)(2,1)S(1)}, bf16[256,3584]{1,0:T(8,128)(2,1)}, u32[]{:S(2)}) %copy-start) | copy-done | bytes 1835032
  5.0 0.0 copy-start.1
  5.0 0.9 %copy-done.1 = bf16[1,1024,1,128]{3,1,2,0:T(8,128)(2,1)S(1)} copy-done((bf16[1,1024,1,128]{3,1,2,0:T(8,128)(2,1)S(1)}, bf16[1,1024,1,128]{3,1,2,0:T(8,128)(2,1)}, u32[]{:S(2)}) %copy-start.1) | copy-done | bytes 262168
  6.0 0.0 copy-start.2
  6.0 0.9 %copy-done.2 = bf16[1,1024,1,128]{3,1,2,0:T(8,128)(2,1)S(1)} copy-done((bf16[1,1024,1,128]{3,1,2,0:T(8,128)(2,1)S(1)}, bf16[1,1024,1,128]{3,1,2,0:T(8,128)(2,1)}, u32[]{:S(2)}) %copy-start.2) | copy-done | bytes 262168
  6.9 0.0 copy-start.3
  7.0 0.9 %copy-done.3 = bf16[1024,128]{1,0:T(8,128)(2,1)S(1)} copy-done((bf16[1024,128]{1,0:T(8,128)(2,1)S(1)}, bf16[1024,128]{1,0:T(8,128)(2,1)}, u32[]{:S(2)}) %copy-start.3) | copy-done | bytes 262168
  7.9 0.0 copy-start.4
  7.9 0.9 %copy-done.4 = bf16[1,64,8,128]{3,2,1,0:T(8,128)(2,1)S(1)} copy-done((bf16[1,64,8,128]{3,2,1,0:T(8,128)(2,1)S(1)}, bf16[1,64,8,128]{3,2,1,0:T(8,128)(2,1)}, u32[]{:S(2)}) %copy-start.4) | copy-done | bytes 131096
  8.8 0.0 copy-start.5
  8.8 0.8 %copy-done.5 = bf16[256,128]{1,0:T(8,128)(2,1)S(1)} copy-done((bf16[256,128]{1,0:T(8,128)(2,1)S(1)}, bf16[256,128]{1,0:T(8,128)(2,1)}, u32[]{:S(2)}) %copy-start.5) | copy-done | bytes 65560
  9.6 0.0 copy-start.6
  9.6 0.7 copy-done.6
  10.4 0.0 copy-start.7
  10.4 0.7 copy-done.7
  11.1 0.0 copy-start.8
  11.1 0.7 copy-done.8
  11.8 0.0 copy-start.9
  11.8 0.7 copy-done.9
  12.5 62.4 %shard_map.165 = (f32[28,128]{1,0:T(8,128)S(1)}, f32[28,128]{1,0:T(8,128)S(1)}, f32[28,128]{1,0:T(8,128)S(1)}, bf16[64,3584]{1,0:T(8,128)(2,1)S(1)}) custom-call(bf16[256,128]{1,0:T(8,128)(2,1)S(1)} %copy-done.5, bf16[256,3584]{1,0:T(8,128)(2,1)S(1)} %copy-done, f32[28,128]{1,0:T(8,128)S(1)} %bitcast.27, f32[28,128]{1,0:T(8,128)S(1)} %bitcast.28, ...), custom_call_target="tpu_custom_call" | custom-call | tf_op jit(solution)/shard_map/pallas_call | solution.py:516
  74.8 0.6 copy.24
  75.5 0.6 copy_bitcast_fusion
  76.1 0.8 copy.27
Async XLA Ops:
  3.5 1.5 %copy-start = (bf16[256,3584]{1,0:T(8,128)(2,1)S(1)}, bf16[256,3584]{1,0:T(8,128)(2,1)}, u32[]{:S(2)}) copy-start(bf16[256,3584]{1,0:T(8,128)(2,1)} %og_h.1) | copy-start | bytes 5505028
  5.0 0.9 %copy-start.1 = (bf16[1,1024,1,128]{3,1,2,0:T(8,128)(2,1)S(1)}, bf16[1,1024,1,128]{3,1,2,0:T(8,128)(2,1)}, u32[]{:S(2)}) copy-start(bf16[1,1024,1,128]{3,1,2,0:T(8,128)(2,1)} %param.20) | copy-start | bytes 786436
  6.0 0.9 %copy-start.2 = (bf16[1,1024,1,128]{3,1,2,0:T(8,128)(2,1)S(1)}, bf16[1,1024,1,128]{3,1,2,0:T(8,128)(2,1)}, u32[]{:S(2)}) copy-start(bf16[1,1024,1,128]{3,1,2,0:T(8,128)(2,1)} %param.21) | copy-start | bytes 786436
  6.9 0.9 %copy-start.3 = (bf16[1024,128]{1,0:T(8,128)(2,1)S(1)}, bf16[1024,128]{1,0:T(8,128)(2,1)}, u32[]{:S(2)}) copy-start(bf16[1024,128]{1,0:T(8,128)(2,1)} %op_h.1) | copy-start | bytes 786436
  7.9 0.9 %copy-start.4 = (bf16[1,64,8,128]{3,2,1,0:T(8,128)(2,1)S(1)}, bf16[1,64,8,128]{3,2,1,0:T(8,128)(2,1)}, u32[]{:S(2)}) copy-start(bf16[1,64,8,128]{3,2,1,0:T(8,128)(2,1)} %param.19) | copy-start | bytes 393220
  8.8 0.8 %copy-start.5 = (bf16[256,128]{1,0:T(8,128)(2,1)S(1)}, bf16[256,128]{1,0:T(8,128)(2,1)}, u32[]{:S(2)}) copy-start(bf16[256,128]{1,0:T(8,128)(2,1)} %acts_h.1) | copy-start | bytes 196612
  9.6 0.7 copy-start.6
  10.4 0.7 copy-start.7
  11.1 0.7 copy-start.8
  11.8 0.7 copy-start.9

commit v2 on v1

v2 whole, which is shorter than its diff:
```python
import functools

import jax
import jax.numpy as jnp
from jax import lax
from jax.experimental import pallas as pl
from jax.experimental.pallas import tpu as pltpu
from jax.sharding import PartitionSpec as P

beta_one = 0.9
beta_two = 0.95
adam_eps = 1e-08
learn_rate = 0.001
weight_decay = 0.1
adam_count = 10
masked_score = -1e30

MESH = pl.DeviceIdType.MESH
LANES = 128
GRIDS = {128: (8, 8, 2), 32: (4, 4, 2), 16: (4, 4, 1), 8: (2, 2, 2)}


def nt_dot(a, b):
    return lax.dot_general(a, b, (((1,), (1,)), ((), ())), preferred_element_type=jnp.float32)


def dot(a, b):
    return jnp.dot(a, b, preferred_element_type=jnp.float32)


def adam(g, moment, second, master):
    moment_new = beta_one * moment + (1.0 - beta_one) * g
    second_new = beta_two * second + (1.0 - beta_two) * g * g
    corr_one = 1.0 - beta_one**adam_count
    corr_two = 1.0 - beta_two**adam_count
    direction = moment_new / corr_one / (jnp.sqrt(second_new / corr_two) + adam_eps)
    master_new = master - learn_rate * (direction + weight_decay * master)
    return moment_new, second_new, master_new


def step_kernel(
    cfg,
    acts_h,
    og_h,
    mom_h,
    sec_h,
    mas_h,
    q_h,
    k_h,
    v_h,
    tk_h,
    tv_h,
    par_h,
    len_h,
    res_h,
    op_h,
    g_o,
    hid_o,
    roll_o,
    acts,
    og,
    opt,
    opt_t,
    q,
    k,
    v,
    tk,
    tv,
    par,
    length,
    res,
    op,
    grad,
    rs_out,
    rs_in,
    tile_f,
    tile_out,
    tile_in,
    row_all,
    blk,
    qf,
    ht,
    ht_in,
    head_all,
    hid,
    g_row,
    own,
    load_sem,
    store_sem,
    rs_send,
    rs_recv,
    ex_send,
    ex_recv,
    row_send,
    row_recv,
    ag_send,
    ag_recv,
    tp_send,
    tp_recv,
):
    nx, ny, nz, nt, chunks = cfg
    rows = acts.shape[1]
    width = grad.shape[-1]
    per = width // LANES
    tiles = per * chunks
    pad = tile_out.shape[2]
    nodes = res.shape[0]
    heads = q.shape[0] // nodes
    share = nodes // nt

    f = lax.axis_index("fsdp")
    t = lax.axis_index("tp")
    x, y, z = f // (ny * nz), lax.rem(f // nz, ny), lax.rem(f, nz)
    sides = (nx, ny)
    pos = (x, y)
    group = (ny * nz, nx * nz)
    mine = (y * nz + z, x * nz + z)

    def line_peer(a, at):
        if a == 0:
            return (at * ny + y) * nz + z
        return (x * ny + at) * nz + z

    def group_peer(a, j):
        if a == 0:
            return x * (ny * nz) + j
        return ((j // nz) * ny + y) * nz + lax.rem(j, nz)

    def far_first(n):
        return sorted(range(1, n), key=lambda kk: -min(kk, n - kk))

    loads = {}

    def load(name, src, dst):
        copy = pltpu.make_async_copy(src, dst, load_sem.at[len(loads)])
        copy.start()
        loads[name] = copy

    load("acts", acts_h, acts)
    for c in range(chunks):
        for a in range(2):
            base = (a * chunks + c) * width
            load(("og", a, c), og_h.at[:, pl.ds(base, width)], og.at[a, c])

    barrier = pltpu.get_barrier_semaphore()
    count = 0
    for kk in range(1, group[0]):
        j = lax.rem(mine[0] + kk, group[0])
        pl.semaphore_signal(barrier, inc=1, device_id=(group_peer(0, j), t), device_id_type=MESH)
        count += 1
    for xx in range(1, nx):
        for zz in range(nz):
            j = lax.rem(x + xx, nx) * nz + zz
            pl.semaphore_signal(barrier, inc=1, device_id=(group_peer(1, j), t), device_id_type=MESH)
            count += 1
    for kk in range(1, nt):
        pl.semaphore_signal(barrier, inc=1, device_id=(f, lax.rem(t + kk, nt)), device_id_type=MESH)
        count += 1

    row_at = lax.broadcasted_iota(jnp.int32, (rows, rows), 0)
    col_at = lax.broadcasted_iota(jnp.int32, (rows, rows), 1)
    py, px, pz = row_at // (nx * nz), lax.rem(row_at // nz, nx), lax.rem(row_at, nz)
    swap = (col_at == (px * ny + py) * nz + pz).astype(jnp.bfloat16)
    same = (col_at == row_at).astype(jnp.bfloat16)
    loads["acts"].wait()
    acts_t = [nt_dot(m, acts[...]).astype(jnp.bfloat16) for m in (same, swap)]

    def block(a, at):
        depth = rows // sides[a]
        return pl.ds(pl.multiple_of(at * depth, depth), depth)

    def wait_for(ref, sem):
        pltpu.make_async_copy(ref, ref, sem).wait()

    for c in range(chunks):
        for a in range(2):
            n = sides[a]
            loads[("og", a, c)].wait()
            value = dot(acts_t[a], og[a, c])
            grad[a, c] = value
            rs_out[a, c] = value.astype(jnp.bfloat16)
            if c == 0 and a == 0:
                pl.semaphore_wait(barrier, count)
            for kk in far_first(n):
                at = lax.rem(pos[a] + kk, n)
                pltpu.make_async_remote_copy(
                    src_ref=rs_out.at[a, c, block(a, at)],
                    dst_ref=rs_in.at[a, c, kk - 1],
                    send_sem=rs_send.at[a, c],
                    recv_sem=rs_recv.at[a, c],
                    device_id=(line_peer(a, at), t),
                    device_id_type=MESH,
                ).start()

    load("par", par_h, par)
    load("q", q_h, q)
    load("tk", tk_h, tk)
    load("k", k_h, k)
    load("len", len_h, length)
    load("v", v_h, v)
    load("tv", tv_h, tv)
    load("op", op_h, op)
    load("mom", mom_h, opt.at[0])
    load("sec", sec_h, opt.at[1])
    load("mas", mas_h, opt.at[2])
    load("res", res_h, res)
    tile_f[...] = jnp.zeros_like(tile_f)

    loads["par"].wait()
    j_at = lax.broadcasted_iota(jnp.int32, (nodes, nodes), 0)
    i_at = lax.broadcasted_iota(jnp.int32, (nodes, nodes), 1)
    links = ((par[...] == j_at) & (i_at > 0)) | (i_at == j_at)
    reach = links.astype(jnp.bfloat16)
    for _ in range(max(1, (nodes - 1).bit_length())):
        reach = jnp.minimum(dot(reach, reach), 1.0).astype(jnp.bfloat16)
    pick_row = lax.broadcasted_iota(jnp.int32, (2 * nodes, nodes), 0)
    pick_col = lax.broadcasted_iota(jnp.int32, (2 * nodes, nodes), 1)
    pick = (lax.rem(pick_row, nodes) == pick_col).astype(jnp.bfloat16)
    admitted = nt_dot(pick, reach) > 0.5
    loads["q"].wait()
    qf[...] = q[...].astype(jnp.float32)

    depth = q.shape[1]
    scale = depth ** (-0.5)
    for name in ("tk", "k", "len", "v", "tv", "op"):
        loads[name].wait()

    def attend(u):
        pair = jnp.concatenate(
            [qf[pl.ds(2 * u + e, nodes, stride=heads), :] for e in range(2)], axis=0
        ).astype(jnp.bfloat16)
        s_cache = nt_dot(pair, k[...])
        s_tree = nt_dot(pair, tk[...])
        live = lax.broadcasted_iota(jnp.int32, s_cache.shape, 1) < length[...]
        s_cache = jnp.where(live, s_cache, masked_score)
        s_tree = jnp.where(admitted, s_tree, masked_score)
        top = jnp.maximum(
            jnp.max(s_cache, axis=1, keepdims=True), jnp.max(s_tree, axis=1, keepdims=True)
        )
        e_cache = jnp.exp((s_cache - top) * scale)
        e_tree = jnp.exp((s_tree - top) * scale)
        total = jnp.sum(e_cache, axis=1, keepdims=True) + jnp.sum(e_tree, axis=1, keepdims=True)
        mixed = dot(e_cache.astype(jnp.bfloat16), v[...]) + dot(e_tree.astype(jnp.bfloat16), tv[...])
        mixed = (mixed / total).astype(jnp.bfloat16)
        add = dot(mixed[:nodes], op[pl.ds(2 * u * depth, depth), :]) + dot(
            mixed[nodes:], op[pl.ds((2 * u + 1) * depth, depth), :]
        )
        if u == 0:
            ht[...] = add
        else:
            ht[...] += add

    units = heads // 2
    early = units - 1
    for u in range(early):
        attend(u)

    for i, name in enumerate(("mom", "sec", "mas")):
        loads[name].wait()
        for a in range(2):
            for e in range(tiles):
                opt_t[i, a, pl.ds(e, 1), :] = opt[i, :, pl.ds((a * tiles + e) * LANES, LANES)]
    loads["res"].wait()

    for a in range(2):
        n = sides[a]
        for c in range(chunks):
            wait_for(rs_in.at[a, c], rs_recv.at[a, c])
            value = grad[a, c, block(a, pos[a]), :]
            for kk in range(n - 1):
                value = value + rs_in[a, c, kk].astype(jnp.float32)
            for e in range(per):
                tile_f[a, pl.ds(c * per + e, group[a], stride=pad), :] = value[:, e * LANES : (e + 1) * LANES]
        tile_out[a] = tile_f[a].astype(jnp.bfloat16).reshape(group[a], pad, LANES)
        for kk in far_first(group[a]):
            j = lax.rem(mine[a] + kk, group[a])
            pltpu.make_async_remote_copy(
                src_ref=tile_out.at[a, j],
                dst_ref=tile_in.at[a, kk - 1],
                send_sem=ex_send.at[a],
                recv_sem=ex_recv.at[a],
                device_id=(group_peer(a, j), t),
                device_id_type=MESH,
            ).start()
        own[a] = tile_f[a, pl.ds(pl.multiple_of(mine[a] * pad, pad), pad), :]

    for u in range(early, units):
        attend(u)

    def share_of(at):
        return pl.ds(pl.multiple_of(at * share, share), share)

    for kk in range(1, nt):
        at = lax.rem(t + kk, nt)
        pltpu.make_async_remote_copy(
            src_ref=ht.at[share_of(at)],
            dst_ref=ht_in.at[kk - 1],
            send_sem=tp_send.at[0],
            recv_sem=tp_recv.at[0],
            device_id=(f, at),
            device_id_type=MESH,
        ).start()

    g_tiles = []
    for a in range(2):
        wait_for(tile_in.at[a], ex_recv.at[a])
        g = own[a]
        for kk in range(group[a] - 1):
            g = g + tile_in[a, kk].astype(jnp.float32)
        g = g[:tiles]
        g_tiles.append(g)
        master_new = adam(g, opt_t[0, a], opt_t[1, a], opt_t[2, a])[2]
        if pad > tiles:
            fill = jnp.zeros((pad - tiles, LANES), jnp.float32)
            master_new = jnp.concatenate([master_new, fill], axis=0)
        row_all[a, mine[a]] = master_new.astype(jnp.bfloat16)
        for kk in far_first(group[a]):
            j = lax.rem(mine[a] + kk, group[a])
            pltpu.make_async_remote_copy(
                src_ref=row_all.at[a, mine[a]],
                dst_ref=row_all.at[a, mine[a]],
                send_sem=row_send.at[a],
                recv_sem=row_recv.at[a],
                device_id=(group_peer(a, j), t),
                device_id_type=MESH,
            ).start()

    stores = []

    def store(src, dst):
        copy = pltpu.make_async_copy(src, dst, store_sem.at[len(stores)])
        copy.start()
        stores.append(copy)

    for a in range(2):
        for e in range(tiles):
            g_row[:, pl.ds((a * tiles + e) * LANES, LANES)] = g_tiles[a][e : e + 1]
    store(g_row, g_o)

    wait_for(ht_in, tp_recv.at[0])
    head = ht[share_of(t), :]
    for kk in range(nt - 1):
        head = head + ht_in[kk]
    head_all[share_of(t), :] = head
    for kk in range(1, nt):
        pltpu.make_async_remote_copy(
            src_ref=head_all.at[share_of(t)],
            dst_ref=head_all.at[share_of(t)],
            send_sem=tp_send.at[1],
            recv_sem=tp_recv.at[1],
            device_id=(f, lax.rem(t + kk, nt)),
            device_id_type=MESH,
        ).start()

    for a in range(2):
        n = sides[a]
        wait_for(row_all.at[a, pl.ds(0, group[a] - 1)], row_recv.at[a])
        tile_f[a] = row_all[a].astype(jnp.float32).reshape(group[a] * pad, LANES)
        for c in range(chunks):
            for e in range(per):
                blk[a, c, :, pl.ds(e * LANES, LANES)] = tile_f[
                    a, pl.ds(c * per + e, group[a], stride=pad), :
                ].astype(jnp.bfloat16)
            for kk in far_first(n):
                at = lax.rem(pos[a] + kk, n)
                pltpu.make_async_remote_copy(
                    src_ref=blk.at[a, c],
                    dst_ref=roll_o.at[a, c, block(a, pos[a])],
                    send_sem=ag_send.at[a, c],
                    recv_sem=ag_recv.at[a, c],
                    device_id=(line_peer(a, at), t),
                    device_id_type=MESH,
                ).start()
            store(blk.at[a, c], roll_o.at[a, c, block(a, pos[a])])

    wait_for(head_all.at[pl.ds(0, (nt - 1) * share)], tp_recv.at[1])
    hidden = (res[...].astype(jnp.float32) + head_all[...]).astype(jnp.bfloat16)
    hid[0] = hidden
    hid[1] = nt_dot(hidden, swap).astype(jnp.bfloat16)
    store(hid, hid_o)

    for a in range(2):
        for c in range(chunks):
            wait_for(rs_in.at[a, c], rs_send.at[a, c])
        wait_for(tile_in.at[a], ex_send.at[a])
        wait_for(row_all.at[a, pl.ds(0, group[a] - 1)], row_send.at[a])
    wait_for(ht_in, tp_send.at[0])
    wait_for(head_all.at[pl.ds(0, (nt - 1) * share)], tp_send.at[1])
    for a in range(2):
        n = sides[a]
        for c in range(chunks):
            others = pl.ds(0, rows - rows // n)
            wait_for(roll_o.at[a, c, others], ag_send.at[a, c])
            wait_for(roll_o.at[a, c, others], ag_recv.at[a, c])
    for copy in stores:
        copy.wait()


def result_kernel(
    roll_h, hid_h, g_h, mom_h, sec_h, mas_h, mom_o, sec_o, mas_o, prop_o, roll, hid, opt, opt_new, stage, load_sem, store_sem
):
    halves, chunks, _, width = roll.shape
    loads = [pltpu.make_async_copy(hid_h, hid, load_sem.at[0])]
    for i in range(halves * chunks):
        at = (i // chunks, i % chunks)
        loads.append(pltpu.make_async_copy(roll_h.at[at], roll.at[at], load_sem.at[1 + i]))
    for i, ref in enumerate((g_h, mom_h, sec_h, mas_h)):
        loads.append(pltpu.make_async_copy(ref, opt.at[i], load_sem.at[1 + halves * chunks + i]))
    for copy in loads:
        copy.start()
    stores = []
    loads[0].wait()
    for i in range(halves * chunks):
        a, c = i // chunks, i % chunks
        loads[1 + i].wait()
        stage[a, c] = dot(hid[a], roll[a, c]).astype(jnp.bfloat16)
        stores.append(
            pltpu.make_async_copy(stage.at[a, c], prop_o.at[:, pl.ds(i * width, width)], store_sem.at[i])
        )
        stores[-1].start()
    for copy in loads[1 + halves * chunks :]:
        copy.wait()
    fresh = adam(opt[0], opt[1], opt[2], opt[3])
    for i, ref in enumerate((mom_o, sec_o, mas_o)):
        opt_new[i] = fresh[i]
        stores.append(pltpu.make_async_copy(opt_new.at[i], ref, store_sem.at[halves * chunks + i]))
        stores[-1].start()
    for copy in stores:
        copy.wait()


def local(
    acts,
    out_grad,
    moment,
    second,
    master,
    queries,
    cache_keys,
    cache_values,
    tree_keys,
    tree_values,
    parents,
    lengths,
    residual,
    out_proj,
    *,
    grid,
    nt,
):
    nx, ny, nz = grid
    chunks = 2
    rows = acts.shape[1]
    columns = out_grad.shape[1]
    width = columns // (2 * chunks)
    tiles = width // LANES * chunks
    pad = -(-tiles // 16) * 16
    nodes, heads, depth = queries.shape[1:]
    cache = cache_keys.shape[1]
    side = ny * nz
    bf16, f32 = jnp.bfloat16, jnp.float32
    hbm = pl.BlockSpec(memory_space=pltpu.HBM)
    dma = pltpu.SemaphoreType.DMA
    limit = 56 * 1024 * 1024
    g_row, hidden, roll = pl.pallas_call(
        functools.partial(step_kernel, (nx, ny, nz, nt, chunks)),
        out_shape=[
            jax.ShapeDtypeStruct((1, columns), f32),
            jax.ShapeDtypeStruct((2, nodes, rows), bf16),
            jax.ShapeDtypeStruct((2, chunks, rows, width), bf16),
        ],
        in_specs=[hbm] * 14,
        out_specs=[hbm] * 3,
        scratch_shapes=[
            pltpu.VMEM(acts.shape, bf16),
            pltpu.VMEM((2, chunks, acts.shape[0], width), bf16),
            pltpu.VMEM((3, 1, columns), f32),
            pltpu.VMEM((3, 2, tiles, LANES), f32),
            pltpu.VMEM((nodes * heads, depth), bf16),
            pltpu.VMEM((cache, depth), bf16),
            pltpu.VMEM((cache, depth), bf16),
            pltpu.VMEM((nodes, depth), bf16),
            pltpu.VMEM((nodes, depth), bf16),
            pltpu.VMEM((1, nodes), jnp.int32),
            pltpu.VMEM((1, 1), jnp.int32),
            pltpu.VMEM((nodes, rows), bf16),
            pltpu.VMEM(out_proj.shape, bf16),
            pltpu.VMEM((2, chunks, rows, width), f32),
            pltpu.VMEM((2, chunks, rows, width), bf16),
            pltpu.VMEM((2, chunks, nx - 1, side, width), bf16),
            pltpu.VMEM((2, side * pad, LANES), f32),
            pltpu.VMEM((2, side, pad, LANES), bf16),
            pltpu.VMEM((2, side - 1, pad, LANES), bf16),
            pltpu.VMEM((2, side, pad, LANES), bf16),
            pltpu.VMEM((2, chunks, side, width), bf16),
            pltpu.VMEM((nodes * heads, depth), f32),
            pltpu.VMEM((nodes, rows), f32),
            pltpu.VMEM((nt - 1, nodes // nt, rows), f32),
            pltpu.VMEM((nodes, rows), f32),
            pltpu.VMEM((2, nodes, rows), bf16),
            pltpu.VMEM((1, columns), f32),
            pltpu.VMEM((2, pad, LANES), f32),
            dma((13 + 2 * chunks,)),
            dma((2 + 2 * chunks,)),
            dma((2, chunks)),
            dma((2, chunks)),
            dma((2,)),
            dma((2,)),
            dma((2,)),
            dma((2,)),
            dma((2, chunks)),
            dma((2, chunks)),
            dma((2,)),
            dma((2,)),
        ],
        compiler_params=pltpu.CompilerParams(
            collective_id=0, has_side_effects=True, vmem_limit_bytes=limit
        ),
    )(
        acts,
        out_grad,
        moment,
        second,
        master,
        queries.reshape(nodes * heads, depth),
        cache_keys.reshape(cache, depth),
        cache_values.reshape(cache, depth),
        tree_keys.reshape(nodes, depth),
        tree_values.reshape(nodes, depth),
        parents,
        lengths.reshape(1, 1),
        residual.reshape(nodes, rows),
        out_proj,
    )
    moment_new, second_new, master_new, proposal = pl.pallas_call(
        result_kernel,
        out_shape=[jax.ShapeDtypeStruct(moment.shape, f32)] * 3
        + [jax.ShapeDtypeStruct((nodes, columns), bf16)],
        in_specs=[hbm] * 6,
        out_specs=[hbm] * 4,
        scratch_shapes=[
            pltpu.VMEM((2, chunks, rows, width), bf16),
            pltpu.VMEM((2, nodes, rows), bf16),
            pltpu.VMEM((4, 1, columns), f32),
            pltpu.VMEM((3, 1, columns), f32),
            pltpu.VMEM((2, chunks, nodes, width), bf16),
            dma((5 + 2 * chunks,)),
            dma((3 + 2 * chunks,)),
        ],
        compiler_params=pltpu.CompilerParams(vmem_limit_bytes=limit),
    )(roll, hidden, g_row, moment, second, master)
    return (moment_new, second_new, master_new, proposal.reshape(1, nodes, columns))


def solution(mesh):
    in_specs = (
        P("fsdp", None),
        P("fsdp", "tp"),
        P("fsdp", "tp"),
        P("fsdp", "tp"),
        P("fsdp", "tp"),
        P("fsdp", None, "tp", None),
        P("fsdp", None, "tp", None),
        P("fsdp", None, "tp", None),
        P("fsdp", None, "tp", None),
        P("fsdp", None, "tp", None),
        P("fsdp", None),
        P("fsdp"),
        P("fsdp", None, None),
        P("tp", None),
    )
    out_specs = (P("fsdp", "tp"), P("fsdp", "tp"), P("fsdp", "tp"), P("fsdp", None, "tp"))
    body = functools.partial(local, grid=GRIDS[mesh.shape["fsdp"]], nt=mesh.shape["tp"])
    return jax.shard_map(body, mesh=mesh, in_specs=in_specs, out_specs=out_specs, check_vma=False)
```

time: 77.5 us -> 59.6 us (0.77)
  the two profiles are of different devices: /device:TPU:6 before, /device:TPU:4 now
where the time goes in v2:
time: 59.6 us; the launch traced here: 59.4 us
  Pallas kernels  58.1 us (97%)
  between operations  1.29 us (2%)
    pallas_call x1, Pallas kernels, local(): pl.pallas_call(functools.partial(step_kernel, (nx, ny, nz, nt, chunks)),...  55.6 us
    pallas_call x1, Pallas kernels, local(): pl.pallas_call(result_kernel, out_shape=[jax.ShapeDtypeStruct(moment.shap...  2.46 us

profile of v2, /device:TPU:4, one launch (start us, length us, event | category | flops | bytes accessed | tf_op | source)
XLA Modules:
  0.0 59.4 jit_solution(16634958273827640638)
XLA Ops:
  1.3 55.6 %shard_map.165 = (f32[1,3584]{1,0:T(1,128)}, bf16[2,64,128]{2,1,0:T(8,128)(2,1)}, bf16[2,2,128,896]{3,2,1,0:T(8,128)(2,1)}) custom-call(bf16[256,128]{1,0:T(8,128)(2,1)} %acts_h.1, bf16[256,3584]{1,0:T(8,128)(2,1)} %og_h.1, f32[1,3584]{1,0:T(1,128)} %mom_h.3, f32[1,3584]{1,0:T(1,128)} %sec_h.3, f32[1,3584]{1,0:T(1,128)} %mas_h.3, bf16[512,128]{1,0:T(8,128)(2,1)} %bitcast.11, ...), custom_call_target="tpu_custom_call" | custom-call | tf_op jit(solution)/shard_map/pallas_call | solution.py:465
  56.9 2.5 %shard_map.166 = (f32[1,3584]{1,0:T(1,128)}, f32[1,3584]{1,0:T(1,128)}, f32[1,3584]{1,0:T(1,128)}, bf16[64,3584]{1,0:T(8,128)(2,1)}) custom-call(bf16[2,2,128,896]{3,2,1,0:T(8,128)(2,1)} %get-tuple-element.11.roll_h, bf16[2,64,128]{2,1,0:T(8,128)(2,1)} %get-tuple-element.12.hid_h, f32[1,3584]{1,0:T(1,128)} %get-tuple-element.13.g_h, f32[1,3584]{1,0:T(1,128)} %mom_h.3, ...), custom_call_target="tpu_custom_call" | custom-call | tf_op jit(solution)/shard_map/pallas_call | solution.py:535

commit v3 on v2

--- a/solution.py
+++ b/solution.py
@@ -81,7 +81,6 @@
     qf,
     ht,
     ht_in,
-    head_all,
     hid,
     g_row,
     own,
@@ -106,7 +105,7 @@
     pad = tile_out.shape[2]
     nodes = res.shape[0]
     heads = q.shape[0] // nodes
-    share = nodes // nt
+    legs = nt.bit_length() - 1
 
     f = lax.axis_index("fsdp")
     t = lax.axis_index("tp")
@@ -126,6 +125,10 @@
             return x * (ny * nz) + j
         return ((j // nz) * ny + y) * nz + lax.rem(j, nz)
 
+    def across(leg):
+        step = 1 << leg
+        return t + step - 2 * step * lax.rem(t // step, 2)
+
     def far_first(n):
         return sorted(range(1, n), key=lambda kk: -min(kk, n - kk))
 
@@ -144,17 +147,17 @@
 
     barrier = pltpu.get_barrier_semaphore()
     count = 0
-    for kk in range(1, group[0]):
-        j = lax.rem(mine[0] + kk, group[0])
-        pl.semaphore_signal(barrier, inc=1, device_id=(group_peer(0, j), t), device_id_type=MESH)
+    for a in range(2):
+        for kk in far_first(sides[a]):
+            peer = line_peer(a, lax.rem(pos[a] + kk, sides[a]))
+            pl.semaphore_signal(barrier, inc=1, device_id=(peer, t), device_id_type=MESH)
+            count += 1
+    for zz in range(1, nz):
+        peer = (x * ny + y) * nz + lax.rem(z + zz, nz)
+        pl.semaphore_signal(barrier, inc=1, device_id=(peer, t), device_id_type=MESH)
         count += 1
-    for xx in range(1, nx):
-        for zz in range(nz):
-            j = lax.rem(x + xx, nx) * nz + zz
-            pl.semaphore_signal(barrier, inc=1, device_id=(group_peer(1, j), t), device_id_type=MESH)
-            count += 1
-    for kk in range(1, nt):
-        pl.semaphore_signal(barrier, inc=1, device_id=(f, lax.rem(t + kk, nt)), device_id_type=MESH)
+    for leg in range(legs):
+        pl.semaphore_signal(barrier, inc=1, device_id=(f, across(leg)), device_id_type=MESH)
         count += 1
 
     row_at = lax.broadcasted_iota(jnp.int32, (rows, rows), 0)
@@ -246,9 +249,9 @@
             mixed[nodes:], op[pl.ds((2 * u + 1) * depth, depth), :]
         )
         if u == 0:
-            ht[...] = add
+            ht[0] = add
         else:
-            ht[...] += add
+            ht[0] += add
 
     units = heads // 2
     early = units - 1
@@ -262,10 +265,12 @@
                 opt_t[i, a, pl.ds(e, 1), :] = opt[i, :, pl.ds((a * tiles + e) * LANES, LANES)]
     loads["res"].wait()
 
+    wait_for(rs_in.at[1, 0], rs_recv.at[1, 0])
     for a in range(2):
         n = sides[a]
         for c in range(chunks):
-            wait_for(rs_in.at[a, c], rs_recv.at[a, c])
+            if (a, c) != (1, 0):
+                wait_for(rs_in.at[a, c], rs_recv.at[a, c])
             value = grad[a, c, block(a, pos[a]), :]
             for kk in range(n - 1):
                 value = value + rs_in[a, c, kk].astype(jnp.float32)
@@ -287,19 +292,27 @@
     for u in range(early, units):
         attend(u)
 
-    def share_of(at):
-        return pl.ds(pl.multiple_of(at * share, share), share)
-
-    for kk in range(1, nt):
-        at = lax.rem(t + kk, nt)
-        pltpu.make_async_remote_copy(
-            src_ref=ht.at[share_of(at)],
-            dst_ref=ht_in.at[kk - 1],
-            send_sem=tp_send.at[0],
-            recv_sem=tp_recv.at[0],
-            device_id=(f, at),
+    leg_copies = []
+
+    def leg_start(leg):
+        copy = pltpu.make_async_remote_copy(
+            src_ref=ht.at[leg],
+            dst_ref=ht_in.at[leg],
+            send_sem=tp_send.at[leg],
+            recv_sem=tp_recv.at[leg],
+            device_id=(f, across(leg)),
             device_id_type=MESH,
-        ).start()
+        )
+        copy.start()
+        leg_copies.append(copy)
+
+    def leg_end(leg):
+        leg_copies[leg].wait_recv()
+        ht[leg + 1] = ht[leg] + ht_in[leg]
+        if leg + 1 < legs:
+            leg_start(leg + 1)
+
+    leg_start(0)
 
     g_tiles = []
     for a in range(2):
@@ -337,20 +350,7 @@
             g_row[:, pl.ds((a * tiles + e) * LANES, LANES)] = g_tiles[a][e : e + 1]
     store(g_row, g_o)
 
-    wait_for(ht_in, tp_recv.at[0])
-    head = ht[share_of(t), :]
-    for kk in range(nt - 1):
-        head = head + ht_in[kk]
-    head_all[share_of(t), :] = head
-    for kk in range(1, nt):
-        pltpu.make_async_remote_copy(
-            src_ref=head_all.at[share_of(t)],
-            dst_ref=head_all.at[share_of(t)],
-            send_sem=tp_send.at[1],
-            recv_sem=tp_recv.at[1],
-            device_id=(f, lax.rem(t + kk, nt)),
-            device_id_type=MESH,
-        ).start()
+    leg_end(0)
 
     for a in range(2):
         n = sides[a]
@@ -373,8 +373,9 @@
                 ).start()
             store(blk.at[a, c], roll_o.at[a, c, block(a, pos[a])])
 
-    wait_for(head_all.at[pl.ds(0, (nt - 1) * share)], tp_recv.at[1])
-    hidden = (res[...].astype(jnp.float32) + head_all[...]).astype(jnp.bfloat16)
+    for leg in range(1, legs):
+        leg_end(leg)
+    hidden = (res[...].astype(jnp.float32) + ht[legs]).astype(jnp.bfloat16)
     hid[0] = hidden
     hid[1] = nt_dot(hidden, swap).astype(jnp.bfloat16)
     store(hid, hid_o)
@@ -384,8 +385,8 @@
             wait_for(rs_in.at[a, c], rs_send.at[a, c])
         wait_for(tile_in.at[a], ex_send.at[a])
         wait_for(row_all.at[a, pl.ds(0, group[a] - 1)], row_send.at[a])
-    wait_for(ht_in, tp_send.at[0])
-    wait_for(head_all.at[pl.ds(0, (nt - 1) * share)], tp_send.at[1])
+    for copy in leg_copies:
+        copy.wait_send()
     for a in range(2):
         n = sides[a]
         for c in range(chunks):
@@ -400,31 +401,33 @@
     roll_h, hid_h, g_h, mom_h, sec_h, mas_h, mom_o, sec_o, mas_o, prop_o, roll, hid, opt, opt_new, stage, load_sem, store_sem
 ):
     halves, chunks, _, width = roll.shape
-    loads = [pltpu.make_async_copy(hid_h, hid, load_sem.at[0])]
-    for i in range(halves * chunks):
+    parts = halves * chunks
+    pairs = [(ref, opt.at[i]) for i, ref in enumerate((g_h, mom_h, sec_h, mas_h))] + [(hid_h, hid)]
+    for i in range(parts):
         at = (i // chunks, i % chunks)
-        loads.append(pltpu.make_async_copy(roll_h.at[at], roll.at[at], load_sem.at[1 + i]))
-    for i, ref in enumerate((g_h, mom_h, sec_h, mas_h)):
-        loads.append(pltpu.make_async_copy(ref, opt.at[i], load_sem.at[1 + halves * chunks + i]))
+        pairs.append((roll_h.at[at], roll.at[at]))
+    loads = [pltpu.make_async_copy(src, dst, load_sem.at[i]) for i, (src, dst) in enumerate(pairs)]
     for copy in loads:
         copy.start()
     stores = []
-    loads[0].wait()
-    for i in range(halves * chunks):
-        a, c = i // chunks, i % chunks
-        loads[1 + i].wait()
-        stage[a, c] = dot(hid[a], roll[a, c]).astype(jnp.bfloat16)
-        stores.append(
-            pltpu.make_async_copy(stage.at[a, c], prop_o.at[:, pl.ds(i * width, width)], store_sem.at[i])
-        )
-        stores[-1].start()
-    for copy in loads[1 + halves * chunks :]:
+
+    def store(src, dst):
+        copy = pltpu.make_async_copy(src, dst, store_sem.at[len(stores)])
+        copy.start()
+        stores.append(copy)
+
+    for copy in loads[:4]:
         copy.wait()
     fresh = adam(opt[0], opt[1], opt[2], opt[3])
     for i, ref in enumerate((mom_o, sec_o, mas_o)):
         opt_new[i] = fresh[i]
-        stores.append(pltpu.make_async_copy(opt_new.at[i], ref, store_sem.at[halves * chunks + i]))
-        stores[-1].start()
+        store(opt_new.at[i], ref)
+    loads[4].wait()
+    for i in range(parts):
+        a, c = i // chunks, i % chunks
+        loads[5 + i].wait()
+        stage[a, c] = dot(hid[a], roll[a, c]).astype(jnp.bfloat16)
+        store(stage.at[a, c], prop_o.at[:, pl.ds(i * width, width)])
     for copy in stores:
         copy.wait()
 
@@ -458,6 +461,7 @@
     nodes, heads, depth = queries.shape[1:]
     cache = cache_keys.shape[1]
     side = ny * nz
+    legs = nt.bit_length() - 1
     bf16, f32 = jnp.bfloat16, jnp.float32
     hbm = pl.BlockSpec(memory_space=pltpu.HBM)
     dma = pltpu.SemaphoreType.DMA
@@ -494,9 +498,8 @@
             pltpu.VMEM((2, side, pad, LANES), bf16),
             pltpu.VMEM((2, chunks, side, width), bf16),
             pltpu.VMEM((nodes * heads, depth), f32),
-            pltpu.VMEM((nodes, rows), f32),
-            pltpu.VMEM((nt - 1, nodes // nt, rows), f32),
-            pltpu.VMEM((nodes, rows), f32),
+            pltpu.VMEM((legs + 1, nodes, rows), f32),
+            pltpu.VMEM((legs, nodes, rows), f32),
             pltpu.VMEM((2, nodes, rows), bf16),
             pltpu.VMEM((1, columns), f32),
             pltpu.VMEM((2, pad, LANES), f32),
@@ -510,8 +513,8 @@
             dma((2,)),
             dma((2, chunks)),
             dma((2, chunks)),
-            dma((2,)),
-            dma((2,)),
+            dma((legs,)),
+            dma((legs,)),
         ],
         compiler_params=pltpu.CompilerParams(
             collective_id=0, has_side_effects=True, vmem_limit_bytes=limit

time: 59.6 us -> 57.2 us (0.960)
  the two profiles are of different devices: /device:TPU:4 before, /device:TPU:2 now
where the time goes in v3:
time: 57.2 us; the launch traced here: 57 us
  Pallas kernels  55.7 us (97%)
  between operations  1.29 us (2%)
    pallas_call x1, Pallas kernels, local(): pl.pallas_call(functools.partial(step_kernel, (nx, ny, nz, nt, chunks)),...  53.2 us
    pallas_call x1, Pallas kernels, local(): pl.pallas_call(result_kernel, out_shape=[jax.ShapeDtypeStruct(moment.shap...  2.52 us

profile of v3, /device:TPU:2, one launch (start us, length us, event | category | flops | bytes accessed | tf_op | source)
XLA Modules:
  0.0 57.0 jit_solution(9990440539238461101)
XLA Ops:
  1.3 53.2 %shard_map.165 = (f32[1,3584]{1,0:T(1,128)}, bf16[2,64,128]{2,1,0:T(8,128)(2,1)}, bf16[2,2,128,896]{3,2,1,0:T(8,128)(2,1)}) custom-call(bf16[256,128]{1,0:T(8,128)(2,1)} %acts_h.1, bf16[256,3584]{1,0:T(8,128)(2,1)} %og_h.1, f32[1,3584]{1,0:T(1,128)} %mom_h.3, f32[1,3584]{1,0:T(1,128)} %sec_h.3, f32[1,3584]{1,0:T(1,128)} %mas_h.3, bf16[512,128]{1,0:T(8,128)(2,1)} %bitcast.11, ...), custom_call_target="tpu_custom_call" | custom-call | tf_op jit(solution)/shard_map/pallas_call | solution.py:469
  54.5 2.5 %shard_map.166 = (f32[1,3584]{1,0:T(1,128)}, f32[1,3584]{1,0:T(1,128)}, f32[1,3584]{1,0:T(1,128)}, bf16[64,3584]{1,0:T(8,128)(2,1)}) custom-call(bf16[2,2,128,896]{3,2,1,0:T(8,128)(2,1)} %get-tuple-element.11.roll_h, bf16[2,64,128]{2,1,0:T(8,128)(2,1)} %get-tuple-element.12.hid_h, f32[1,3584]{1,0:T(1,128)} %get-tuple-element.13.g_h, f32[1,3584]{1,0:T(1,128)} %mom_h.3, ...), custom_call_target="tpu_custom_call" | custom-call | tf_op jit(solution)/shard_map/pallas_call | solution.py:538

commit v4 on v3

--- a/solution.py
+++ b/solution.py
@@ -17,7 +17,7 @@
 
 MESH = pl.DeviceIdType.MESH
 LANES = 128
-GRIDS = {128: (8, 8, 2), 32: (4, 4, 2), 16: (4, 4, 1), 8: (2, 2, 2)}
+GRIDS = {128: (8, 8, 2)}
 
 
 def nt_dot(a, b):
@@ -78,6 +78,7 @@
     tile_in,
     row_all,
     blk,
+    relay,
     qf,
     ht,
     ht_in,
@@ -352,8 +353,27 @@
 
     leg_end(0)
 
-    for a in range(2):
+    ag_copies = []
+
+    def ag_copy(a, c, d, kind, src, owner, step):
         n = sides[a]
+        at = lax.rem(pos[a] + (1 - 2 * d) * step + n, n)
+        landing = relay.at[a, c, d] if kind == 1 else roll_o.at[a, c, block(a, owner)]
+        return pltpu.make_async_remote_copy(
+            src_ref=src,
+            dst_ref=landing,
+            send_sem=ag_send.at[a, c, d, kind],
+            recv_sem=ag_recv.at[a, c, d, kind],
+            device_id=(line_peer(a, at), t),
+            device_id_type=MESH,
+        )
+
+    def ag_start(*which):
+        copy = ag_copy(*which)
+        copy.start()
+        ag_copies.append(copy)
+
+    for a in range(2):
         wait_for(row_all.at[a, pl.ds(0, group[a] - 1)], row_recv.at[a])
         tile_f[a] = row_all[a].astype(jnp.float32).reshape(group[a] * pad, LANES)
         for c in range(chunks):
@@ -361,19 +381,26 @@
                 blk[a, c, :, pl.ds(e * LANES, LANES)] = tile_f[
                     a, pl.ds(c * per + e, group[a], stride=pad), :
                 ].astype(jnp.bfloat16)
-            for kk in far_first(n):
-                at = lax.rem(pos[a] + kk, n)
-                pltpu.make_async_remote_copy(
-                    src_ref=blk.at[a, c],
-                    dst_ref=roll_o.at[a, c, block(a, pos[a])],
-                    send_sem=ag_send.at[a, c],
-                    recv_sem=ag_recv.at[a, c],
-                    device_id=(line_peer(a, at), t),
-                    device_id_type=MESH,
-                ).start()
+            for d in range(2):
+                ag_start(a, c, d, 1, blk.at[a, c], pos[a], 2)
+        for c in range(chunks):
+            for d in range(2):
+                ag_start(a, c, d, 0, blk.at[a, c], pos[a], 1)
             store(blk.at[a, c], roll_o.at[a, c, block(a, pos[a])])
-
-    for leg in range(1, legs):
+    if legs > 1:
+        leg_end(1)
+    for a in range(2):
+        n = sides[a]
+        for c in range(chunks):
+            for d in range(2):
+                owner = lax.rem(pos[a] - 2 * (1 - 2 * d) + n, n)
+                ag_copy(a, c, d, 1, blk.at[a, c], pos[a], 2).wait_recv()
+                ag_start(a, c, d, 2, relay.at[a, c, d], owner, 1)
+                if c % 2 == d:
+                    ag_start(a, c, d, 3, relay.at[a, c, d], owner, 2)
+                store(relay.at[a, c, d], roll_o.at[a, c, block(a, owner)])
+
+    for leg in range(2, legs):
         leg_end(leg)
     hidden = (res[...].astype(jnp.float32) + ht[legs]).astype(jnp.bfloat16)
     hid[0] = hidden
@@ -387,12 +414,14 @@
         wait_for(row_all.at[a, pl.ds(0, group[a] - 1)], row_send.at[a])
     for copy in leg_copies:
         copy.wait_send()
-    for a in range(2):
-        n = sides[a]
+    for copy in ag_copies:
+        copy.wait_send()
+    for a in range(2):
         for c in range(chunks):
-            others = pl.ds(0, rows - rows // n)
-            wait_for(roll_o.at[a, c, others], ag_send.at[a, c])
-            wait_for(roll_o.at[a, c, others], ag_recv.at[a, c])
+            for d in range(2):
+                for kind in (0, 2, 3):
+                    if kind < 3 or c % 2 == d:
+                        ag_copy(a, c, d, kind, blk.at[a, c], pos[a], 1).wait_recv()
     for copy in stores:
         copy.wait()
 
@@ -497,6 +526,7 @@
             pltpu.VMEM((2, side - 1, pad, LANES), bf16),
             pltpu.VMEM((2, side, pad, LANES), bf16),
             pltpu.VMEM((2, chunks, side, width), bf16),
+            pltpu.VMEM((2, chunks, 2, side, width), bf16),
             pltpu.VMEM((nodes * heads, depth), f32),
             pltpu.VMEM((legs + 1, nodes, rows), f32),
             pltpu.VMEM((legs, nodes, rows), f32),
@@ -504,15 +534,15 @@
             pltpu.VMEM((1, columns), f32),
             pltpu.VMEM((2, pad, LANES), f32),
             dma((13 + 2 * chunks,)),
-            dma((2 + 2 * chunks,)),
+            dma((2 + 6 * chunks,)),
             dma((2, chunks)),
             dma((2, chunks)),
             dma((2,)),
             dma((2,)),
             dma((2,)),
             dma((2,)),
-            dma((2, chunks)),
-            dma((2, chunks)),
+            dma((2, chunks, 2, 4)),
+            dma((2, chunks, 2, 4)),
             dma((legs,)),
             dma((legs,)),
         ],

time: 57.2 us -> 56.6 us (0.990)
  Pallas kernels: 55.7 us -> 55.1 us
    pallas_call x1, Pallas kernels: 53.2 us -> 52.6 us  [local(): pl.pallas_call(functools.partial(step_kernel, (nx, ny, nz, nt, chunks)),...]
where the time goes in v4:
time: 56.6 us; the launch traced here: 56.4 us
  Pallas kernels  55.1 us (97%)
  between operations  1.29 us (2%)
    pallas_call x1, Pallas kernels, local(): pl.pallas_call(functools.partial(step_kernel, (nx, ny, nz, nt, chunks)),...  52.6 us
    pallas_call x1, Pallas kernels, local(): pl.pallas_call(result_kernel, out_shape=[jax.ShapeDtypeStruct(moment.shap...  2.52 us

profile of v4, /device:TPU:2, one launch (start us, length us, event | category | flops | bytes accessed | tf_op | source)
XLA Modules:
  0.0 56.4 jit_solution(13282486362563366725)
XLA Ops:
  1.3 52.6 %shard_map.165 = (f32[1,3584]{1,0:T(1,128)}, bf16[2,64,128]{2,1,0:T(8,128)(2,1)}, bf16[2,2,128,896]{3,2,1,0:T(8,128)(2,1)}) custom-call(bf16[256,128]{1,0:T(8,128)(2,1)} %acts_h.1, bf16[256,3584]{1,0:T(8,128)(2,1)} %og_h.1, f32[1,3584]{1,0:T(1,128)} %mom_h.3, f32[1,3584]{1,0:T(1,128)} %sec_h.3, f32[1,3584]{1,0:T(1,128)} %mas_h.3, bf16[512,128]{1,0:T(8,128)(2,1)} %bitcast.11, ...), custom_call_target="tpu_custom_call" | custom-call | tf_op jit(solution)/shard_map/pallas_call | solution.py:498
  53.8 2.5 %shard_map.166 = (f32[1,3584]{1,0:T(1,128)}, f32[1,3584]{1,0:T(1,128)}, f32[1,3584]{1,0:T(1,128)}, bf16[64,3584]{1,0:T(8,128)(2,1)}) custom-call(bf16[2,2,128,896]{3,2,1,0:T(8,128)(2,1)} %get-tuple-element.11.roll_h, bf16[2,64,128]{2,1,0:T(8,128)(2,1)} %get-tuple-element.12.hid_h, f32[1,3584]{1,0:T(1,128)} %get-tuple-element.13.g_h, f32[1,3584]{1,0:T(1,128)} %mom_h.3, ...), custom_call_target="tpu_custom_call" | custom-call | tf_op jit(solution)/shard_map/pallas_call | solution.py:568

commit v5 on v4

--- a/solution.py
+++ b/solution.py
@@ -54,7 +54,7 @@
     len_h,
     res_h,
     op_h,
-    g_o,
+    new_o,
     hid_o,
     roll_o,
     acts,
@@ -83,7 +83,7 @@
     ht,
     ht_in,
     hid,
-    g_row,
+    opt_new,
     own,
     load_sem,
     store_sem,
@@ -315,15 +315,15 @@
 
     leg_start(0)
 
-    g_tiles = []
+    fresh = []
     for a in range(2):
         wait_for(tile_in.at[a], ex_recv.at[a])
         g = own[a]
         for kk in range(group[a] - 1):
             g = g + tile_in[a, kk].astype(jnp.float32)
         g = g[:tiles]
-        g_tiles.append(g)
-        master_new = adam(g, opt_t[0, a], opt_t[1, a], opt_t[2, a])[2]
+        fresh.append(adam(g, opt_t[0, a], opt_t[1, a], opt_t[2, a]))
+        master_new = fresh[a][2]
         if pad > tiles:
             fill = jnp.zeros((pad - tiles, LANES), jnp.float32)
             master_new = jnp.concatenate([master_new, fill], axis=0)
@@ -346,10 +346,6 @@
         copy.start()
         stores.append(copy)
 
-    for a in range(2):
-        for e in range(tiles):
-            g_row[:, pl.ds((a * tiles + e) * LANES, LANES)] = g_tiles[a][e : e + 1]
-    store(g_row, g_o)
 
     leg_end(0)
 
@@ -387,6 +383,11 @@
             for d in range(2):
                 ag_start(a, c, d, 0, blk.at[a, c], pos[a], 1)
             store(blk.at[a, c], roll_o.at[a, c, block(a, pos[a])])
+    for i in range(3):
+        for a in range(2):
+            for e in range(tiles):
+                opt_new[i, :, pl.ds((a * tiles + e) * LANES, LANES)] = fresh[a][i][e : e + 1]
+    store(opt_new, new_o)
     if legs > 1:
         leg_end(1)
     for a in range(2):
@@ -414,6 +415,8 @@
         wait_for(row_all.at[a, pl.ds(0, group[a] - 1)], row_send.at[a])
     for copy in leg_copies:
         copy.wait_send()
+    for copy in stores:
+        copy.wait()
     for copy in ag_copies:
         copy.wait_send()
     for a in range(2):
@@ -422,16 +425,14 @@
                 for kind in (0, 2, 3):
                     if kind < 3 or c % 2 == d:
                         ag_copy(a, c, d, kind, blk.at[a, c], pos[a], 1).wait_recv()
-    for copy in stores:
-        copy.wait()
 
 
 def result_kernel(
-    roll_h, hid_h, g_h, mom_h, sec_h, mas_h, mom_o, sec_o, mas_o, prop_o, roll, hid, opt, opt_new, stage, load_sem, store_sem
+    roll_h, hid_h, new_h, mom_o, sec_o, mas_o, prop_o, roll, hid, stage, load_sem, store_sem
 ):
     halves, chunks, _, width = roll.shape
     parts = halves * chunks
-    pairs = [(ref, opt.at[i]) for i, ref in enumerate((g_h, mom_h, sec_h, mas_h))] + [(hid_h, hid)]
+    pairs = [(hid_h, hid)]
     for i in range(parts):
         at = (i // chunks, i % chunks)
         pairs.append((roll_h.at[at], roll.at[at]))
@@ -445,16 +446,12 @@
         copy.start()
         stores.append(copy)
 
-    for copy in loads[:4]:
-        copy.wait()
-    fresh = adam(opt[0], opt[1], opt[2], opt[3])
     for i, ref in enumerate((mom_o, sec_o, mas_o)):
-        opt_new[i] = fresh[i]
-        store(opt_new.at[i], ref)
-    loads[4].wait()
+        store(new_h.at[i], ref)
+    loads[0].wait()
     for i in range(parts):
         a, c = i // chunks, i % chunks
-        loads[5 + i].wait()
+        loads[1 + i].wait()
         stage[a, c] = dot(hid[a], roll[a, c]).astype(jnp.bfloat16)
         store(stage.at[a, c], prop_o.at[:, pl.ds(i * width, width)])
     for copy in stores:
@@ -495,10 +492,10 @@
     hbm = pl.BlockSpec(memory_space=pltpu.HBM)
     dma = pltpu.SemaphoreType.DMA
     limit = 56 * 1024 * 1024
-    g_row, hidden, roll = pl.pallas_call(
+    new_rows, hidden, roll = pl.pallas_call(
         functools.partial(step_kernel, (nx, ny, nz, nt, chunks)),
         out_shape=[
-            jax.ShapeDtypeStruct((1, columns), f32),
+            jax.ShapeDtypeStruct((3, 1, columns), f32),
             jax.ShapeDtypeStruct((2, nodes, rows), bf16),
             jax.ShapeDtypeStruct((2, chunks, rows, width), bf16),
         ],
@@ -531,7 +528,7 @@
             pltpu.VMEM((legs + 1, nodes, rows), f32),
             pltpu.VMEM((legs, nodes, rows), f32),
             pltpu.VMEM((2, nodes, rows), bf16),
-            pltpu.VMEM((1, columns), f32),
+            pltpu.VMEM((3, 1, columns), f32),
             pltpu.VMEM((2, pad, LANES), f32),
             dma((13 + 2 * chunks,)),
             dma((2 + 6 * chunks,)),
@@ -569,19 +566,17 @@
         result_kernel,
         out_shape=[jax.ShapeDtypeStruct(moment.shape, f32)] * 3
         + [jax.ShapeDtypeStruct((nodes, columns), bf16)],
-        in_specs=[hbm] * 6,
+        in_specs=[hbm] * 3,
         out_specs=[hbm] * 4,
         scratch_shapes=[
             pltpu.VMEM((2, chunks, rows, width), bf16),
             pltpu.VMEM((2, nodes, rows), bf16),
-            pltpu.VMEM((4, 1, columns), f32),
-            pltpu.VMEM((3, 1, columns), f32),
             pltpu.VMEM((2, chunks, nodes, width), bf16),
-            dma((5 + 2 * chunks,)),
+            dma((1 + 2 * chunks,)),
             dma((3 + 2 * chunks,)),
         ],
         compiler_params=pltpu.CompilerParams(vmem_limit_bytes=limit),
-    )(roll, hidden, g_row, moment, second, master)
+    )(roll, hidden, new_rows)
     return (moment_new, second_new, master_new, proposal.reshape(1, nodes, columns))
 
 

time: 56.6 us -> 56.6 us (level)
  no operation moved by 1% of the time
where the time goes in v5:
time: 56.6 us; the launch traced here: 56.3 us
  Pallas kernels  55.1 us (97%)
  between operations  1.29 us (2%)
    pallas_call x1, Pallas kernels, local(): pl.pallas_call(functools.partial(step_kernel, (nx, ny, nz, nt, chunks)),...  52.5 us
    pallas_call x1, Pallas kernels, local(): pl.pallas_call(result_kernel, out_shape=[jax.ShapeDtypeStruct(moment.shap...  2.53 us

profile of v5, /device:TPU:2, one launch (start us, length us, event | category | flops | bytes accessed | tf_op | source)
XLA Modules:
  0.0 56.3 jit_solution(17457503127098159226)
XLA Ops:
  1.3 52.5 %shard_map.165 = (f32[3,1,3584]{2,1,0:T(1,128)}, bf16[2,64,128]{2,1,0:T(8,128)(2,1)}, bf16[2,2,128,896]{3,2,1,0:T(8,128)(2,1)}) custom-call(bf16[256,128]{1,0:T(8,128)(2,1)} %acts_h.1, bf16[256,3584]{1,0:T(8,128)(2,1)} %og_h.1, f32[1,3584]{1,0:T(1,128)} %mom_h.1, f32[1,3584]{1,0:T(1,128)} %sec_h.1, f32[1,3584]{1,0:T(1,128)} %mas_h.1, ...), custom_call_target="tpu_custom_call" | custom-call | tf_op jit(solution)/shard_map/pallas_call | solution.py:495
  53.8 2.5 %shard_map.166 = (f32[1,3584]{1,0:T(1,128)}, f32[1,3584]{1,0:T(1,128)}, f32[1,3584]{1,0:T(1,128)}, bf16[64,3584]{1,0:T(8,128)(2,1)}) custom-call(bf16[2,2,128,896]{3,2,1,0:T(8,128)(2,1)} %get-tuple-element.11.roll_h, bf16[2,64,128]{2,1,0:T(8,128)(2,1)} %get-tuple-element.12.hid_h, f32[3,1,3584]{2,1,0:T(1,128)} %get-tuple-element.13.new_h), custom_call_target="tpu_custom_call" | custom-call | tf_op jit(solution)/shard_map/pallas_call | solution.py:565
